TPU v7x, 32 devices: a whole 2x2x4 slice. The times are simulated.
32 devices in a mesh: head: 4 (over z), vocab: 8 (over y, x, core).
Axes of the slice: x: 2, y: 2, z: 4, core: 2. Of those that a mesh axis runs over, the one named last changes fastest.
Arguments:
- queries: bfloat16 [16, 8192], P(None, 'head')
- key_cache: bfloat16 [256, 1024], P('vocab', 'head')
- value_cache: bfloat16 [256, 1024], P('vocab', 'head'), may hold values from -6 to 6
- visible_len: int32 [16], replicated, may hold values from 128 to 241
- targets: int32 [16], replicated, may hold values from 0 to 28671
- final_scale: float32 [16], replicated, may hold values from 4 to 40
- w_out: bfloat16 [8192, 8192], P('head', 'vocab'), may hold values from -0.5 to 0.5
- unembed: bfloat16 [8192, 28672], P(None, ('head', 'vocab'))
Outputs:
- target_logit: float32 [64, 16], replicated
- log_norm: float32 [64, 16], replicated
All inputs are finite; a program needn't handle non-finite values.
Results may differ from a plain program's by a relative error of at most 0.0043.
Values may be sent and summed in bfloat16 or wider, within the bound.
A program may use at most 128 MiB of HBM per device.

v0:
```python
import jax
import jax.numpy as jnp
from jax import lax
from jax.sharding import PartitionSpec as P

H = 64
KVH = 8
HD = 128


NEG_FILL = -1e30


def combined_all(part, axis, combine):
    gathered = jax.tree.map(lambda a: lax.all_gather(a, axis), part)

    def take(source):
        return jax.tree.map(lambda a: lax.dynamic_index_in_dim(a, source, 0, False), gathered)

    return lax.fori_loop(
        1, lax.axis_size(axis), lambda source, state: combine(state, take(source)), take(0)
    )


def combine_softmax(former, latter):
    new_peak = jnp.maximum(former[0], latter[0])
    former_weight = jnp.exp(former[0] - new_peak)
    latter_weight = jnp.exp(latter[0] - new_peak)
    new_total = former[1] * former_weight + latter[1] * latter_weight
    new_summed = former[2] * former_weight[..., None] + latter[2] * latter_weight[..., None]
    return (new_peak, new_total, new_summed)


def body(queries, key_cache, value_cache, visible_len, targets, final_scale, w_out, unembed):
    keys_local = key_cache.shape[0]
    vocab_count = lax.axis_size("vocab")
    context = keys_local * vocab_count
    query_count = queries.shape[0]
    kv_local = key_cache.shape[1] // HD
    group_size = H // KVH
    heads_local = kv_local * group_size
    qgrid = queries.reshape(query_count, kv_local, group_size, HD)
    kgrid = key_cache.reshape(keys_local, kv_local, HD)
    vgrid = value_cache.reshape(keys_local, kv_local, HD)
    scores = jnp.einsum(
        "sngd,knd->ngsk", qgrid, kgrid, preferred_element_type=jnp.float32
    ) * HD ** (-0.5)
    key_pos = lax.axis_index("vocab") * keys_local + jnp.arange(keys_local, dtype=jnp.int32)
    query_pos = context - query_count + jnp.arange(query_count, dtype=jnp.int32)
    visible = (key_pos[None, :] <= query_pos[:, None]) & (
        key_pos[None, :] > (query_pos - visible_len)[:, None]
    )
    masked = jnp.where(visible, scores, NEG_FILL)
    row_peak = jnp.max(masked, axis=-1)
    weights = jnp.where(visible, jnp.exp(masked - row_peak[..., None]), 0.0)
    row_total = jnp.sum(weights, axis=-1)
    summed = jnp.einsum(
        "ngsk,knd->ngsd", weights, vgrid.astype(jnp.float32), precision=lax.Precision.HIGHEST
    )
    row_peak, row_total, summed = combined_all(
        (row_peak, row_total, summed), "vocab", combine_softmax
    )
    mixed = (
        (summed / row_total[..., None]).astype(jnp.bfloat16).reshape(heads_local, query_count, HD)
    )
    width_local = w_out.shape[1]
    projection = w_out.reshape(heads_local, HD, width_local)
    contrib = jnp.einsum("hse,hed->hsd", mixed, projection, preferred_element_type=jnp.float32)
    scaled = (contrib * final_scale[None, :, None]).astype(jnp.bfloat16)
    voc_local = unembed.shape[1]
    all_heads = lax.all_gather(scaled, "head", axis=0, tiled=True)
    piece = lax.all_gather(all_heads, "vocab", axis=2, tiled=True)
    logits = jnp.dot(piece.reshape(-1, piece.shape[2]), unembed, preferred_element_type=jnp.float32)
    first_col = (lax.axis_index("head") * vocab_count + lax.axis_index("vocab")) * voc_local
    col_index = first_col + jnp.arange(voc_local, dtype=jnp.int32)
    target_hits = (targets[:, None] == col_index[None, :]).astype(jnp.float32)
    logit_grid = logits.reshape(H, query_count, voc_local)
    picked = jnp.sum(logit_grid * target_hits[None], axis=-1)
    local_peak = jnp.max(logit_grid, axis=-1)
    global_peak = lax.pmax(local_peak, ("head", "vocab"))
    local_total = jnp.sum(jnp.exp(logit_grid - global_peak[..., None]), axis=-1)
    global_total, target_logit = lax.psum((local_total, picked), ("head", "vocab"))
    return (target_logit, global_peak + jnp.log(global_total))


def solution(mesh):
    return jax.shard_map(
        body,
        mesh=mesh,
        in_specs=(
            P(None, "head"),
            P("vocab", "head"),
            P("vocab", "head"),
            P(),
            P(),
            P(),
            P("head", "vocab"),
            P(None, ("head", "vocab")),
        ),
        out_specs=(P(), P()),
        check_vma=False,
    )
```

profile of v0, /device:TPU:0, one launch (start us, length us, event | category | flops | bytes accessed | tf_op | source)
XLA Modules:
  0.0 302.1 jit_solution(8628537697901946218)
XLA Ops:
  7.9 0.8 copy.25
  8.8 0.7 reshape.69
  9.5 0.7 reshape.71
  10.5 0.9 fusion.8
  11.7 10.7 %all-gather.1 = f32[16,8,16]{2,1,0:T(8,128)S(1)} all-gather(f32[2,8,16]{2,1,0:T(8,128)S(1)} %fusion.9), channel_id=3, replica_groups=mesh['head'=4,'vocab'=8] {'vocab'}, dimensions={0}, use_global_device_ids=true | all-gather | bytes 9216 | tf_op jit(solution)/shard_map/all_gather | solution.py:15
  22.4 9.2 %all-gather = f32[16,8,16]{2,1,0:T(8,128)S(1)} all-gather(f32[2,8,16]{2,1,0:T(8,128)S(1)} %get-tuple-element.205), channel_id=2, replica_groups=mesh['head'=4,'vocab'=8] {'vocab'}, dimensions={0}, use_global_device_ids=true | all-gather | bytes 9216 | tf_op jit(solution)/shard_map/all_gather | solution.py:15
  31.6 6.2 %all-gather.11.cloned.1.call-done = f32[16,8,16,128]{3,2,1,0:T(8,128)} async-done(((f32[2,8,16,128]{3,2,1,0:T(8,128)}), f32[16,8,16,128]{3,2,1,0:T(8,128)}) %all-gather.11.cloned.1.call-update) | async-done | bytes 1048592 | tf_op jit(solution)/shard_map/all_gather | solution.py:15
  37.8 0.9 slice.8
  38.7 7.9 %while.19 = (s32[]{:T(128)}, f32[2,8,16]{2,1,0:T(8,128)S(1)}, f32[2,8,16]{2,1,0:T(8,128)S(1)}, f32[2,8,16,128]{3,2,1,0:T(8,128)S(1)}, f32[8,2,8,16]{3,2,1,0:T(8,...) while((s32[]{:T(128)}, f32[2,8,16]{2,1,0:T(8,128)S(1)}, ...), condition=%wide.region_3.4_spmd, body=%wide.region_2.3_spmd.sunk | while | flops 99845 | bytes 403607 | solution.py:20
  38.8 1.1 fusion.27
  39.9 1.1 fusion.27
  41.0 1.1 fusion.27
  42.1 1.1 fusion.27
  43.3 1.1 fusion.27
  44.4 1.1 fusion.27
  45.5 1.1 fusion.27
  46.7 3.6 %fusion.5 = bf16[16,16,1024]{2,1,0:T(8,128)(2,1)} fusion(bf16[16,16,128]{2,1,0:T(8,128)(2,1)S(1)} %bitcast.43, bf16[16,128,1024]{2,1,0:T(8,128)(2,1)} %bitcast.41, f32[16]{0:T(128)S(1)} %copy-done), kind=kOutput, calls=%fused_computation.13 | convolution fusion | flops 67633152 | bytes 4784192 | tf_op jit(solution)/shard_map/hse,hed->hsd/dot_general | solution.py:68
  50.5 46.0 %all-gather.7.cloned.1.call-done = bf16[64,16,1024]{2,1,0:T(8,128)(2,1)} async-done(((bf16[16,16,1024]{2,1,0:T(8,128)(2,1)}), bf16[64,16,1024]{2,1,0:T(8,128)(2,1)}) %all-gather.7.cloned.1.call-update) | async-done | bytes 2097168 | tf_op jit(solution)/shard_map/all_gather | solution.py:71
  96.6 90.4 %all-gather.9.cloned.1.call-done = bf16[64,16,8192]{2,1,0:T(8,128)(2,1)} async-done(((bf16[64,16,1024]{2,1,0:T(8,128)(2,1)}), bf16[64,16,8192]{2,1,0:T(8,128)(2,1)}) %all-gather.9.cloned.1.call-update) | async-done | bytes 16777232 | tf_op jit(solution)/shard_map/all_gather | solution.py:72
  187.0 23.3 %fusion.20 = (f32[64,16]{1,0:T(8,128)S(1)}, f32[64,16,896]{2,1,0:T(8,128)}) fusion(bf16[64,16,8192]{2,1,0:T(8,128)(2,1)} %all-gather.9.cloned.1.call-done, bf16[8192,896]{1,0:T(8,128)(2,1)} %param.17), kind=kOutput, calls=%fused_computation.36 | convolution fusion | flops 15033302016 | bytes 35131392 | tf_op jit(solution)/shard_map/dot_general | solution.py:73
  210.3 39.4 %pmax.7 = f32[64,16]{1,0:T(8,128)S(1)} all-reduce(f32[64,16]{1,0:T(8,128)S(1)} %get-tuple-element.207), channel_id=1, replica_groups=mesh['head'=4,'vocab'=8] {'head','vocab'}, use_global_device_ids=true, to_apply=%region_7.8 | all-reduce | flops 1024 | bytes 8192 | tf_op jit(solution)/shard_map/pmax | solution.py:80
  249.8 2.9 exponential_reduce_fusion
  252.7 41.5 %all-reduce = (f32[64,16]{1,0:T(8,128)S(1)}, f32[64,16]{1,0:T(8,128)S(1)}) all-reduce(f32[64,16]{1,0:T(8,128)S(1)} %get-tuple-element.184, f32[64,16]{1,0:T(8,128)S(1)} %get-tuple-element.183), channel_id=1, replica_groups=mesh['head'=4,'vocab'=8] {'head','vocab'}, use_global_device_ids=true, to_apply=%region_5.6 | all-reduce | flops 2048 | bytes 16384 | tf_op jit(solution)/shard_map/psum | solution.py:82
  294.2 0.7 copy.18
  (29 shorter events, 2.4 us)
Async XLA Ops:
  7.2 39.6 %copy-start = (f32[16]{0:T(128)S(1)}, f32[16]{0:T(128)}, u32[]{:S(2)}) copy-start(f32[16]{0:T(128)} %param.15) | copy-start | bytes 196
  7.2 30.6 %all-gather.11.cloned.1.call-start = ((), (), s32[]{:S(2)}) async-start(), calls=%async_computation.2 | async-start | bytes 1179648 | tf_op jit(solution)/shard_map/all_gather | solution.py:15
  11.5 85.0 %all-gather.7.cloned.1.call-start = ((), (), s32[]{:S(2)}) async-start(), calls=%async_computation | async-start | bytes 2621440 | tf_op jit(solution)/shard_map/all_gather | solution.py:71
  46.6 49.9 %copy-start.1 = (s32[16]{0:T(128)S(1)}, s32[16]{0:T(128)}, u32[]{:S(2)}) copy-start(s32[16]{0:T(128)} %param.14) | copy-start | bytes 196
  50.4 136.6 %all-gather.9.cloned.1.call-start = ((), (), s32[]{:S(2)}) async-start(), calls=%async_computation.1 | async-start | bytes 18874368 | tf_op jit(solution)/shard_map/all_gather | solution.py:72
Sparse Core Ops, SparseCore 0:
  11.6 26.1 all-gather.10
  50.5 45.9 all-gather.6
  98.4 88.5 all-gather.8
where the time goes:
time: 303 us; the launch traced here: 302 us
  waiting for transfers between devices  143 us (47%)
  blocking collectives  101 us (33%)
  matrix products  28.1 us (9%)
  between operations  13.9 us (5%)
  other arithmetic  11.7 us (4%)
  local copies, waits for them, and re-layouts  4.57 us (2%)
    all_gather x1, waiting for transfers between devices, body(): piece = lax.all_gather(all_heads, 'vocab', axis=2, tiled=True)  90.4 us
    all_gather x1, waiting for transfers between devices, body(): all_heads = lax.all_gather(scaled, 'head', axis=0, tiled=True)  46 us
    psum x1, blocking collectives, body(): lax.psum((local_total, picked), ('head', 'vocab'))  41.5 us
    pmax x1, blocking collectives, body(): global_peak = lax.pmax(local_peak, ('head', 'vocab'))  39.4 us
    dot_general x1, matrix products, body(): jnp.dot(piece.reshape(-1, piece.shape[2]), unembed, preferred_element_typ...  23.3 us
    all_gather x2, blocking collectives, combined_all(): gathered = jax.tree.map(lambda a: lax.all_gather(a, axis), part)  19.9 us
    add x7, other arithmetic, combine_softmax(): former[2] * former_weight[..., None] + latter[2] * latter_weight[..., None]  7.51 us
    all_gather x1, waiting for transfers between devices, combined_all(): gathered = jax.tree.map(lambda a: lax.all_gather(a, axis), part)  6.21 us
  transfers between devices with their start and end apart: 3, of which 3 were waited for; matrix products, arithmetic and copies ran while one was open for 0% of the time, Pallas kernels for 0%

commit v1 on v0

v1 whole, which is shorter than its diff:
```python
import functools

import jax
import jax.numpy as jnp
from jax import lax
from jax.experimental import pallas as pl
from jax.experimental.pallas import tpu as pltpu
from jax.sharding import PartitionSpec as P

H = 64
KVH = 8
HD = 128
GROUP = H // KVH
NEG_FILL = -1e30
MESH = pl.DeviceIdType.MESH
F32 = jnp.float32
BF16 = jnp.bfloat16


def column_tiles(width, tile=256):
    return [(at, min(tile, width - at)) for at in range(0, width, tile)]


def kernel(
    n_h, n_v,
    vis_ref, tgt_ref, fs_ref, q_ref, k_ref, v_ref, w_hbm, u_hbm,
    tl_ref, ln_ref,
    w_buf, u_buf, blocks, acc, kbuf, vbuf, cols, st_all, st_z,
    w_sem, u_sem, kv_send, kv_recv, recv, z_send, x_send, y_send, x_fwd, y_fwd, sib_send,
    st_send, st_recv, sz_send, sz_recv,
):
    z = lax.axis_index("head")
    v = lax.axis_index("vocab")
    n_1 = n_v // 4
    core = lax.rem(v, 2)
    p0 = lax.rem(v // 2, 2)
    p1 = v // 4

    def rel(a, b, e):
        return (lax.rem(p1 + a, n_1) * 2 + lax.rem(p0 + b, 2)) * 2 + lax.rem(core + e, 2)

    sib = rel(0, 0, 1)
    x_nb = rel(0, 1, 0)
    queries = q_ref.shape[0]
    keys = k_ref.shape[0]
    context = keys * n_v
    kv_local = k_ref.shape[1] // HD
    heads = kv_local * GROUP
    rows, width = blocks.shape[2], blocks.shape[3]
    half_rows = rows // 2
    voc = u_buf.shape[1]

    w_copy = pltpu.make_async_copy(w_hbm, w_buf, w_sem)
    w_copy.start()
    u_copy = pltpu.make_async_copy(u_hbm, u_buf, u_sem)
    u_copy.start()

    barrier = pltpu.get_barrier_semaphore()
    for j in range(1, n_v):
        pl.semaphore_signal(barrier, inc=1, device_id=(z, lax.rem(v + j, n_v)), device_id_type=MESH)
    for j in range(1, n_h):
        pl.semaphore_signal(barrier, inc=1, device_id=(lax.rem(z + j, n_h), v), device_id_type=MESH)
    pl.semaphore_wait(barrier, n_v - 1 + n_h - 1)

    def kv_copies(j):
        peer = lax.rem(v + j, n_v)
        return [
            pltpu.make_async_remote_copy(
                src_ref=ref, dst_ref=buf.at[v], send_sem=kv_send.at[i, j],
                recv_sem=kv_recv.at[i, v], device_id=(z, peer), device_id_type=MESH,
            )
            for i, (ref, buf) in enumerate(((k_ref, kbuf), (v_ref, vbuf)))
        ]

    def kv_arrived(j):
        peer = lax.rem(v + j, n_v)
        for i, (ref, buf) in enumerate(((k_ref, kbuf), (v_ref, vbuf))):
            pltpu.make_async_remote_copy(
                src_ref=ref, dst_ref=buf.at[peer], send_sem=kv_send.at[i, j],
                recv_sem=kv_recv.at[i, peer], device_id=(z, peer), device_id_type=MESH,
            ).wait_recv()

    for j in range(1, n_v):
        for copy in kv_copies(j):
            copy.start()
    kbuf[v] = k_ref[...]
    vbuf[v] = v_ref[...]

    def block_copy(zp, vp, half, sem, device):
        part = blocks.at[zp, vp, pl.ds(half * half_rows, half_rows)]
        return pltpu.make_async_remote_copy(
            src_ref=part, dst_ref=part, send_sem=sem, recv_sem=recv.at[zp, vp, half],
            device_id=device, device_id_type=MESH,
        )

    def arrived(zp, vp, half):
        block_copy(zp, vp, half, sib_send.at[0, 0, half], (z, sib)).wait_recv()

    def sib_copy(zp, a, b, half):
        return block_copy(zp, rel(a, b, 0), half, sib_send.at[zp, a * 2 + b, half], (z, sib))

    def plane_copies(zp, half):
        return [block_copy(zp, v, half, x_send.at[zp, half], (z, x_nb))] + [
            block_copy(zp, v, half, y_send.at[zp, a, half], (z, rel(a, 0, 0)))
            for a in range(1, n_1)
        ]

    def x_forwards(zp):
        return [
            block_copy(zp, rel(a, 0, 0), 1, x_fwd.at[zp, a], (z, x_nb)) for a in range(1, n_1)
        ]

    def y_forwards(zp):
        return [
            block_copy(zp, x_nb, 0, y_fwd.at[zp, a], (z, rel(a, 0, 0))) for a in range(1, n_1)
        ]

    def along_head(zp, half, act):
        @pl.when((zp <= z) & (z < n_h - 1))
        def _():
            act(block_copy(zp, v, half, z_send.at[zp, 0, half], (z + 1, v)))

        @pl.when((zp >= z) & (z > 0))
        def _():
            act(block_copy(zp, v, half, z_send.at[zp, 1, half], (z - 1, v)))

    def start(copy):
        copy.start()

    def wait_send(copy):
        copy.wait_send()

    def spread(zp, half):
        along_head(zp, half, start)
        for copy in plane_copies(zp, half):
            copy.start()
        sib_copy(zp, 0, 0, half).start()

    query_row = lax.broadcasted_iota(jnp.int32, (queries, context), 0)
    key_pos = lax.broadcasted_iota(jnp.int32, (queries, context), 1)
    row_one = lax.broadcasted_iota(jnp.int32, (queries, 1), 0)
    seen = jnp.zeros((queries, context), jnp.int32)
    scale = jnp.zeros((queries, 1), F32)
    for s in range(queries):
        seen = jnp.where(query_row == s, vis_ref[s], seen)
        scale = jnp.where(row_one == s, fs_ref[s], scale)
    query_pos = context - queries + query_row
    visible_one = ((key_pos <= query_pos) & (key_pos > query_pos - seen)).astype(jnp.int32)
    visible = jnp.concatenate([visible_one] * GROUP, axis=0) > 0

    for j in range(1, n_v):
        kv_arrived(j)
    gap = jnp.zeros((queries, HD), BF16)
    for n in range(kv_local):
        q = jnp.concatenate(
            [q_ref[:, (n * GROUP + g) * HD:(n * GROUP + g + 1) * HD] for g in range(GROUP)], axis=0
        )
        k = kbuf[:, :, n * HD:(n + 1) * HD].reshape(context, HD)
        val = vbuf[:, :, n * HD:(n + 1) * HD].reshape(context, HD)
        scores = lax.dot_general(
            q, k, (((1,), (1,)), ((), ())), preferred_element_type=F32
        ) * HD ** (-0.5)
        masked = jnp.where(visible, scores, NEG_FILL)
        peak = jnp.max(masked, axis=-1, keepdims=True)
        weights = jnp.where(visible, jnp.exp(masked - peak), 0.0)
        total = jnp.sum(weights, axis=-1, keepdims=True)
        high = weights.astype(BF16)
        rest = weights - high.astype(F32)
        mid = rest.astype(BF16)
        low = (rest - mid.astype(F32)).astype(BF16)
        summed = (
            jnp.dot(low, val, preferred_element_type=F32)
            + jnp.dot(mid, val, preferred_element_type=F32)
            + jnp.dot(high, val, preferred_element_type=F32)
        )
        mixed = (summed / total).astype(BF16)
        if n == 0:
            w_copy.wait()
        for g in range(0, GROUP, 2):
            first = mixed[g * queries:(g + 1) * queries]
            second = mixed[(g + 1) * queries:(g + 2) * queries]
            pair = jnp.concatenate(
                [
                    jnp.concatenate([first, gap], axis=1),
                    jnp.concatenate([gap, second], axis=1),
                ],
                axis=0,
            )
            head = n * GROUP + g
            contrib = jnp.dot(
                pair, w_buf[head * HD:(head + 2) * HD], preferred_element_type=F32
            )
            scaled = contrib * jnp.concatenate([scale, scale], axis=0)
            blocks[z, v, pl.ds(head * queries, 2 * queries)] = scaled.astype(BF16)
            if head + 2 == heads // 2:
                spread(z, 0)
            if head + 2 == heads:
                spread(z, 1)

    first_col = (z * n_v + v) * voc
    col = lax.broadcasted_iota(jnp.int32, (queries, voc), 1) + first_col
    voc_row = lax.broadcasted_iota(jnp.int32, (queries, voc), 0)
    wanted = jnp.full((queries, voc), -1, jnp.int32)
    for s in range(queries):
        wanted = jnp.where(voc_row == s, tgt_ref[s], wanted)
    hits = jnp.where(wanted == col, 1.0, 0.0).astype(F32)

    def source(k):
        below, above = z, n_h - 1 - z
        both = jnp.minimum(below, above)
        paired = k <= 2 * both
        distance = jnp.where(paired, (k + 1) // 2, k - both)
        upward = jnp.where(paired, lax.rem(k, 2) == 1, above > below)
        return z + jnp.where(upward, distance, -distance)

    def multiply(zp, vp, fresh=False):
        depth = pl.ds(pl.multiple_of(vp * width, width), width)
        for at, size in column_tiles(voc):
            part = jnp.dot(
                blocks[zp, vp], u_buf[depth, at:at + size], preferred_element_type=F32
            )
            if fresh:
                acc[zp, :, at:at + size] = part
            else:
                acc[zp, :, at:at + size] += part

    def st_copies(zp):
        return [
            pltpu.make_async_remote_copy(
                src_ref=st_all.at[v, zp], dst_ref=st_all.at[v, zp], send_sem=st_send.at[j, zp],
                recv_sem=st_recv.at[v, zp], device_id=(z, lax.rem(v + j, n_v)), device_id_type=MESH,
            )
            for j in range(1, n_v)
        ]

    def finish(zp):
        for a in range(1, n_1):
            for half in range(2):
                arrived(zp, rel(a, 1, 0), half)
                sib_copy(zp, a, 1, half).start()
        for a in range(1, n_1):
            multiply(zp, rel(a, 1, 0))
        for a in range(1, n_1):
            for half in range(2):
                arrived(zp, rel(a, 1, 1), half)
            multiply(zp, rel(a, 1, 1))
        lane = lax.broadcasted_iota(jnp.int32, (2 * queries, HD), 1)
        for at in range(0, rows, 2 * queries):
            logits = acc[zp, at:at + 2 * queries]
            peak = jnp.max(logits, axis=-1, keepdims=True)
            total = jnp.sum(jnp.exp(logits - peak), axis=-1, keepdims=True)
            picked = jnp.sum(
                logits * jnp.concatenate([hits, hits], axis=0), axis=-1, keepdims=True
            )
            cols[at:at + 2 * queries] = jnp.where(
                lane == 0, peak, jnp.where(lane == 1, total, picked)
            )
        st_all[v, zp] = cols[...].T[:8]
        for copy in st_copies(zp):
            copy.start()

    u_copy.wait()

    def step(k, carry):
        zk = source(k)
        after = source(k + 1)
        for half in range(2):
            @pl.when(k + 1 < n_h)
            def _():
                arrived(after, v, half)
                spread(after, half)

            if half == 0:
                multiply(zk, v, fresh=True)
            arrived(zk, x_nb, half)
            if half == 0:
                for copy in y_forwards(zk):
                    copy.start()
            sib_copy(zk, 0, 1, half).start()
            for a in range(1, n_1):
                arrived(zk, rel(a, 0, 0), half)
            if half == 1:
                for copy in x_forwards(zk):
                    copy.start()
            for a in range(1, n_1):
                sib_copy(zk, a, 0, half).start()

        multiply(zk, x_nb)
        for a in range(1, n_1):
            multiply(zk, rel(a, 0, 0))
        for a, b in [(0, 0), (0, 1)] + [(a, 0) for a in range(1, n_1)]:
            for half in range(2):
                arrived(zk, rel(a, b, 1), half)
            multiply(zk, rel(a, b, 1))

        @pl.when(k > 0)
        def _():
            finish(source(k - 1))

        return carry

    lax.fori_loop(0, n_h, step, 0)
    finish(source(n_h - 1))

    def st_wait(j, zp):
        peer = lax.rem(v + j, n_v)
        pltpu.make_async_remote_copy(
            src_ref=st_all.at[peer, zp], dst_ref=st_all.at[peer, zp], send_sem=st_send.at[j, zp],
            recv_sem=st_recv.at[peer, zp], device_id=(z, peer), device_id_type=MESH,
        ).wait_recv()

    for j in range(1, n_v):
        for zp in range(n_h):
            st_wait(j, zp)

    def merged(parts):
        peak = functools.reduce(jnp.maximum, [part[:, 0:1] for part in parts])
        total = sum(part[:, 1:2] * jnp.exp(part[:, 0:1] - peak) for part in parts)
        picked = sum(part[:, 2:3] for part in parts)
        return peak, total, picked

    peak, total, picked = merged([st_all[i] for i in range(n_v)])
    st_z[z] = jnp.concatenate([peak, total, picked, jnp.zeros((n_h, 5, rows), F32)], axis=1)

    def sz_copy(j, slot):
        peer = lax.rem(z + j, n_h)
        return pltpu.make_async_remote_copy(
            src_ref=st_z.at[slot], dst_ref=st_z.at[slot], send_sem=sz_send.at[j],
            recv_sem=sz_recv.at[slot], device_id=(peer, v), device_id_type=MESH,
        )

    for j in range(1, n_h):
        sz_copy(j, z).start()
    for j in range(1, n_h):
        sz_copy(j, lax.rem(z + j, n_h)).wait_recv()
    peak, total, picked = merged([st_z[i] for i in range(n_h)])
    tl_ref[...] = picked
    ln_ref[...] = peak + jnp.log(total)

    for j in range(1, n_h):
        sz_copy(j, z).wait_send()
    for j in range(1, n_v):
        for copy in kv_copies(j):
            copy.wait_send()

    def drain(zp, carry):
        for half in range(2):
            along_head(zp, half, wait_send)
            for copy in plane_copies(zp, half):
                copy.wait_send()
            for a in range(n_1):
                for b in range(2):
                    sib_copy(zp, a, b, half).wait_send()
        for copy in x_forwards(zp) + y_forwards(zp) + st_copies(zp):
            copy.wait_send()
        return carry

    lax.fori_loop(0, n_h, drain, 0)


def solution(mesh):
    n_h, n_v = mesh.shape["head"], mesh.shape["vocab"]

    def body(queries, key_cache, value_cache, visible_len, targets, final_scale, w_out, unembed):
        count = queries.shape[0]
        rows = w_out.shape[0] // HD * count
        width = w_out.shape[1]
        voc = unembed.shape[1]
        n_1 = n_v // 4
        smem = pl.BlockSpec(memory_space=pltpu.SMEM)
        vmem = pl.BlockSpec(memory_space=pltpu.VMEM)
        hbm = pl.BlockSpec(memory_space=pl.ANY)
        dma = pltpu.SemaphoreType.DMA
        target_logit, log_norm = pl.pallas_call(
            functools.partial(kernel, n_h, n_v),
            out_shape=[jax.ShapeDtypeStruct((n_h, 1, rows), F32)] * 2,
            in_specs=[smem, smem, smem, vmem, vmem, vmem, hbm, hbm],
            out_specs=[vmem, vmem],
            scratch_shapes=[
                pltpu.VMEM(w_out.shape, BF16),
                pltpu.VMEM(unembed.shape, BF16),
                pltpu.VMEM((n_h, n_v, rows, width), BF16),
                pltpu.VMEM((n_h, rows, voc), F32),
                pltpu.VMEM((n_v,) + key_cache.shape, BF16),
                pltpu.VMEM((n_v,) + value_cache.shape, BF16),
                pltpu.VMEM((rows, HD), F32),
                pltpu.VMEM((n_v, n_h, 8, rows), F32),
                pltpu.VMEM((n_h, n_h, 8, rows), F32),
                dma,
                dma,
                dma((2, n_v)),
                dma((2, n_v)),
                dma((n_h, n_v, 2)),
                dma((n_h, 2, 2)),
                dma((n_h, 2)),
                dma((n_h, n_1, 2)),
                dma((n_h, n_1)),
                dma((n_h, n_1)),
                dma((n_h, n_v // 2, 2)),
                dma((n_v, n_h)),
                dma((n_v, n_h)),
                dma((n_h,)),
                dma((n_h,)),
            ],
            compiler_params=pltpu.CompilerParams(
                collective_id=0, has_side_effects=True, vmem_limit_bytes=58 * 2 ** 20
            ),
        )(visible_len, targets, final_scale, queries, key_cache, value_cache, w_out, unembed)
        return target_logit.reshape(H, count), log_norm.reshape(H, count)

    return jax.shard_map(
        body,
        mesh=mesh,
        in_specs=(
            P(None, "head"),
            P("vocab", "head"),
            P("vocab", "head"),
            P(),
            P(),
            P(),
            P("head", "vocab"),
            P(None, ("head", "vocab")),
        ),
        out_specs=(P(), P()),
        check_vma=False,
    )
```

time: 303 us -> 100 us (0.33)
  waiting for transfers between devices: 143 us -> 0 us
  blocking collectives: 101 us -> 0 us
  Pallas kernels: 0 us -> 96.3 us
  matrix products: 28.1 us -> 0 us
  between operations: 13.9 us -> 0.64 us
  other arithmetic: 11.7 us -> 1.4 us
  local copies, waits for them, and re-layouts: 4.57 us -> 1.51 us
    all_gather x3 -> x0, waiting for transfers between devices: 143 us -> none  [the longest x1 90.4 us: body(): piece = lax.all_gather(all_heads, 'vocab', axis=2, tiled=True)]
    pallas_call x0 -> x1, Pallas kernels: none -> 96.3 us  [body(): pl.pallas_call(functools.partial(kernel, n_h, n_v), out_shape=[jax.ShapeD...]
    psum x1 -> x0, blocking collectives: 41.5 us -> none  [body(): lax.psum((local_total, picked), ('head', 'vocab'))]
    pmax x1 -> x0, blocking collectives: 39.4 us -> none  [body(): global_peak = lax.pmax(local_peak, ('head', 'vocab'))]
    dot_general x4 -> x0, matrix products: 28.1 us -> none  [the longest x1 23.3 us: body(): jnp.dot(piece.reshape(-1, piece.shape[2]), unembed, preferred_element_typ...]
    all_gather x2 -> x0, blocking collectives: 19.9 us -> none  [combined_all(): gathered = jax.tree.map(lambda a: lax.all_gather(a, axis), part)]
    add x18 -> x0, other arithmetic: 8.33 us -> none  [the longest x7 7.51 us: combine_softmax(): former[2] * former_weight[..., None] + latter[2] * latter_weight[..., None]]
    reduce_sum x2 -> x0, other arithmetic: 3.14 us -> none  [the longest x1 2.94 us: body(): local_total = jnp.sum(jnp.exp(logit_grid - global_peak[..., None]), axis=-1)]
  transfers between devices with their start and end apart: 3 -> 0, of which waited for: 3 -> 0; matrix products, arithmetic and copies ran while one was open for 0% -> 0% of each run, Pallas kernels for 0% -> 0%
where the time goes in v1:
time: 100 us; the launch traced here: 99.9 us
  Pallas kernels  96.3 us (96%)
  local copies, waits for them, and re-layouts  1.51 us (2%)
  other arithmetic  1.4 us (1%)
    pallas_call x1, Pallas kernels, body(): pl.pallas_call(functools.partial(kernel, n_h, n_v), out_shape=[jax.ShapeD...  96.3 us

profile of v1, /device:TPU:0, one launch (start us, length us, event | category | flops | bytes accessed | tf_op | source)
XLA Modules:
  0.0 99.9 jit_solution(1493202515141616336)
XLA Ops:
  0.6 96.3 %shard_map.95 = (f32[4,1,256]{2,1,0:T(1,128)}, f32[4,1,256]{2,1,0:T(1,128)}) custom-call(s32[16]{0:T(128)} %vis_ref.1, s32[16]{0:T(128)} %tgt_ref.1, f32[16]{0:T(128)} %fs_ref.1, bf16[16,2048]{1,0:T(8,128)(2,1)} %q_ref.1, bf16[32,256]{1,0:T(8,128)(2,1)} %k_ref.1, bf16[32,256]{1,0:T(8,128)(2,1)} %v_ref.1, bf16[2048,1024]{1,0:T(8,128)(2,1)} %w_hbm.1, ...), custom_call_target="tpu_custom_call" | custom-call | tf_op jit(solution)/shard_map/pallas_call | solution.py:374
  97.0 0.7 reduce
  97.7 0.7 reduce.1
  98.4 0.1 reshape.11
  98.4 0.7 copy.13
  99.1 0.1 reshape.10
  99.2 0.7 copy.12

commit v2 on v1

--- a/solution.py
+++ b/solution.py
@@ -26,7 +26,7 @@
     vis_ref, tgt_ref, fs_ref, q_ref, k_ref, v_ref, w_hbm, u_hbm,
     tl_ref, ln_ref,
     w_buf, u_buf, blocks, acc, kbuf, vbuf, cols, st_all, st_z,
-    w_sem, u_sem, kv_send, kv_recv, recv, z_send, x_send, y_send, x_fwd, y_fwd, sib_send,
+    w_sem, u_sem, kv_send, kv_recv, recv, z_send, x_send, y_send, x_fwd, y_fwd, sib_send, diag_send,
     st_send, st_recv, sz_send, sz_recv,
 ):
     z = lax.axis_index("head")
@@ -123,6 +123,23 @@
         @pl.when((zp >= z) & (z > 0))
         def _():
             act(block_copy(zp, v, half, z_send.at[zp, 1, half], (z - 1, v)))
+
+    def apart(zp):
+        return jnp.where(zp > z, zp - z, z - zp)
+
+    def over_plane(zp):
+        return (apart(zp) == 0) | (apart(zp) > 2)
+
+    def diagonal_along_head(zp, a, half, act):
+        vp = rel(a, 1, 0)
+
+        @pl.when((zp <= z) & (z < n_h - 1) & (apart(zp) < 2))
+        def _():
+            act(block_copy(zp, vp, half, diag_send.at[zp, a, half], (z + 1, v)))
+
+        @pl.when((zp >= z) & (z > 0) & (apart(zp) < 2))
+        def _():
+            act(block_copy(zp, vp, half, diag_send.at[zp, n_1 + a, half], (z - 1, v)))
 
     def start(copy):
         copy.start()
@@ -237,6 +254,7 @@
         for a in range(1, n_1):
             for half in range(2):
                 arrived(zp, rel(a, 1, 0), half)
+                diagonal_along_head(zp, a, half, start)
                 sib_copy(zp, a, 1, half).start()
         for a in range(1, n_1):
             multiply(zp, rel(a, 1, 0))
@@ -274,14 +292,20 @@
                 multiply(zk, v, fresh=True)
             arrived(zk, x_nb, half)
             if half == 0:
-                for copy in y_forwards(zk):
-                    copy.start()
+                @pl.when(over_plane(zk))
+                def _():
+                    for copy in y_forwards(zk):
+                        copy.start()
+
             sib_copy(zk, 0, 1, half).start()
             for a in range(1, n_1):
                 arrived(zk, rel(a, 0, 0), half)
             if half == 1:
-                for copy in x_forwards(zk):
-                    copy.start()
+                @pl.when(over_plane(zk))
+                def _():
+                    for copy in x_forwards(zk):
+                        copy.start()
+
             for a in range(1, n_1):
                 sib_copy(zk, a, 0, half).start()
 
@@ -334,8 +358,10 @@
     for j in range(1, n_h):
         sz_copy(j, lax.rem(z + j, n_h)).wait_recv()
     peak, total, picked = merged([st_z[i] for i in range(n_h)])
-    tl_ref[...] = picked
-    ln_ref[...] = peak + jnp.log(total)
+    norm = peak + jnp.log(total)
+    for i in range(n_h):
+        tl_ref[i:i + 1] = picked[i]
+        ln_ref[i:i + 1] = norm[i]
 
     for j in range(1, n_h):
         sz_copy(j, z).wait_send()
@@ -351,7 +377,15 @@
             for a in range(n_1):
                 for b in range(2):
                     sib_copy(zp, a, b, half).wait_send()
-        for copy in x_forwards(zp) + y_forwards(zp) + st_copies(zp):
+            for a in range(1, n_1):
+                diagonal_along_head(zp, a, half, wait_send)
+
+        @pl.when(over_plane(zp))
+        def _():
+            for copy in x_forwards(zp) + y_forwards(zp):
+                copy.wait_send()
+
+        for copy in st_copies(zp):
             copy.wait_send()
         return carry
 
@@ -373,7 +407,7 @@
         dma = pltpu.SemaphoreType.DMA
         target_logit, log_norm = pl.pallas_call(
             functools.partial(kernel, n_h, n_v),
-            out_shape=[jax.ShapeDtypeStruct((n_h, 1, rows), F32)] * 2,
+            out_shape=[jax.ShapeDtypeStruct((n_h, rows), F32)] * 2,
             in_specs=[smem, smem, smem, vmem, vmem, vmem, hbm, hbm],
             out_specs=[vmem, vmem],
             scratch_shapes=[
@@ -397,6 +431,7 @@
                 dma((n_h, n_1)),
                 dma((n_h, n_1)),
                 dma((n_h, n_v // 2, 2)),
+                dma((n_h, 2 * n_1, 2)),
                 dma((n_v, n_h)),
                 dma((n_v, n_h)),
                 dma((n_h,)),

time: 100 us -> 101 us (1.010)
  other arithmetic: 1.4 us -> 0 us
  local copies, waits for them, and re-layouts: 1.51 us -> 2.85 us
    pallas_call x2 -> x0, other arithmetic: 1.4 us -> none  [body(): pl.pallas_call(functools.partial(kernel, n_h, n_v), out_shape=[jax.ShapeD...]
    reshape x2, local copies, waits for them, and re-layouts: 0.16 us -> 1.5 us  [body(): return (target_logit.reshape(H, count), log_norm.reshape(H, count))]
where the time goes in v2:
time: 101 us
  Pallas kernels  97.2 us (96%)
  local copies, waits for them, and re-layouts  2.85 us (3%)
    pallas_call x1, Pallas kernels, body(): pl.pallas_call(functools.partial(kernel, n_h, n_v), out_shape=[jax.ShapeD...  97.2 us

profile of v2, /device:TPU:0, one launch (start us, length us, event | category | flops | bytes accessed | tf_op | source)
XLA Modules:
  0.0 100.7 jit_solution(4867601660515219097)
XLA Ops:
  0.6 97.2 %shard_map.95 = (f32[4,256]{1,0:T(4,128)}, f32[4,256]{1,0:T(4,128)}) custom-call(s32[16]{0:T(128)} %vis_ref.1, s32[16]{0:T(128)} %tgt_ref.1, f32[16]{0:T(128)} %fs_ref.1, bf16[16,2048]{1,0:T(8,128)(2,1)} %q_ref.1, bf16[32,256]{1,0:T(8,128)(2,1)} %k_ref.1, bf16[32,256]{1,0:T(8,128)(2,1)} %v_ref.1, bf16[2048,1024]{1,0:T(8,128)(2,1)} %w_hbm.1, ...), custom_call_target="tpu_custom_call" | custom-call | tf_op jit(solution)/shard_map/pallas_call | solution.py:408
  97.9 0.7 reshape.10
  98.6 0.7 copy.12
  99.3 0.7 reshape.11
  100.0 0.7 copy.13
